TPU v7x, 32 devices: a whole 2x2x4 slice. The times are simulated.
32 devices in a mesh: dp: 4 (over z), mp: 8 (over y, x, core).
Axes of the slice: x: 2, y: 2, z: 4, core: 2. Of those that a mesh axis runs over, the one named last changes fastest.
Arguments:
- grad_parts: bfloat16 [4, 8, 512, 10240], P('dp', None, 'mp'), may hold values from -1.1953125 to 1.1953125
- statistics: float32 [2, 5, 4, 8, 512, 512], P(None, None, 'dp', 'mp'), as said below
- prior_roots: bfloat16 [2, 5, 4, 8, 512, 512], P(None, None, 'dp', 'mp'), as said below
- block_order: int32 [160], replicated, may hold values from 0 to 159, each once
Outputs:
- new_statistics: float32 [2, 5, 4, 8, 512, 512], P(None, None, 'dp', 'mp')
- new_roots: bfloat16 [2, 5, 4, 8, 512, 512], P(None, None, 'dp', 'mp')
- update: bfloat16 [8, 512, 10240], P(None, 'mp')
Inputs may be any that keep to these rules, and one draw needn't show every extreme that they name: block_order holds every block index once; the block at position j goes to slot position j of the statistics' leading dimensions. `statistics`: each matrix is symmetric positive definite. `prior_roots`: each matrix is symmetric.
All inputs are finite; a program needn't handle non-finite values.
Results may differ from a plain program's by a relative error of at most 0.014.
Values may be sent and summed in bfloat16 or wider, within the bound.
A program may use at most 192 MiB of HBM per device.

v0:
```python
import jax
import jax.numpy as jnp
from jax import lax
from jax.sharding import PartitionSpec as P

ITERS = 2


DECAY = 0.95


def inverse_root(matrix):
    identity = jnp.eye(matrix.shape[0], dtype=jnp.float32)
    magnitude = jnp.sqrt(jnp.sum(matrix * matrix)) + 1e-06
    current = matrix / magnitude
    iterate = identity * magnitude ** (-0.25)
    for iteration in range(ITERS):
        factor = (5.0 * identity - current) / 4.0
        iterate = jnp.dot(iterate, factor, precision=lax.Precision.HIGHEST)
        if iteration + 1 < ITERS:
            square = jnp.dot(factor, factor, precision=lax.Precision.HIGHEST)
            fourth = jnp.dot(square, square, precision=lax.Precision.HIGHEST)
            current = jnp.dot(fourth, current, precision=lax.Precision.HIGHEST)
    return iterate


def owner_work(operands):
    left_stat, right_stat, left_root, right_root, block_grad = operands
    left_gram = jnp.dot(block_grad, block_grad.T, preferred_element_type=jnp.float32)
    right_gram = jnp.dot(block_grad.T, block_grad, preferred_element_type=jnp.float32)
    new_left = DECAY * left_stat + (1.0 - DECAY) * left_gram
    new_right = DECAY * right_stat + (1.0 - DECAY) * right_gram
    scaled = jnp.dot(left_root, block_grad, preferred_element_type=jnp.float32).astype(jnp.bfloat16)
    update = jnp.dot(scaled, right_root, preferred_element_type=jnp.float32).astype(jnp.bfloat16)
    root_left = inverse_root(new_left).astype(jnp.bfloat16)
    root_right = inverse_root(new_right).astype(jnp.bfloat16)
    return (new_left, new_right, root_left, root_right, update)


def shards(grad_parts, statistics, prior_roots, block_order):
    data_count = lax.axis_size("dp")
    model_count = lax.axis_size("mp")
    block_size = statistics.shape[-1]
    slot_count = statistics.shape[1]
    block_rows = grad_parts.shape[1]
    row_count = grad_parts.shape[2]
    block_cols = grad_parts.shape[3] // block_size
    block_count = block_order.shape[0]
    positions = slot_count * data_count * model_count
    position = jnp.arange(positions, dtype=jnp.int32)
    is_live = position < block_count
    chosen = jnp.where(is_live, block_order[jnp.minimum(position, block_count - 1)], 0)
    grad_tiles = grad_parts.reshape(block_rows, row_count, block_cols, block_size)
    pieces = grad_tiles[chosen // block_cols, :, chosen % block_cols, :]
    pieces = jnp.where(is_live[:, None, None], pieces, jnp.zeros_like(pieces))
    pieces = pieces.reshape(slot_count, data_count, model_count, row_count, block_size)
    received = lax.all_to_all(pieces, "mp", split_axis=2, concat_axis=3, tiled=True)
    summed = lax.psum_scatter(received, "dp", scatter_dimension=1, tiled=True).astype(jnp.float32)
    owned_grad = summed.astype(jnp.bfloat16).reshape(slot_count, block_size, block_size)
    stats_local = statistics.reshape(2, slot_count, block_size, block_size)
    roots_local = prior_roots.reshape(2, slot_count, block_size, block_size)
    new_left, new_right, root_left, root_right, updates = lax.map(
        owner_work, (stats_local[0], stats_local[1], roots_local[0], roots_local[1], owned_grad)
    )
    device_flat = lax.axis_index("dp") * model_count + lax.axis_index("mp")
    slot_live = (
        jnp.arange(slot_count, dtype=jnp.int32) * (data_count * model_count) + device_flat
        < block_count
    )
    slot_mask = slot_live[:, None, None]
    new_statistics = jnp.stack(
        [jnp.where(slot_mask, new_left, 0.0), jnp.where(slot_mask, new_right, 0.0)]
    ).reshape(statistics.shape)
    root_zeros = jnp.zeros_like(root_left)
    new_roots = jnp.stack(
        [jnp.where(slot_mask, root_left, root_zeros), jnp.where(slot_mask, root_right, root_zeros)]
    ).reshape(prior_roots.shape)
    outgoing = updates.reshape(slot_count, 1, 1, block_size, block_size)
    returned = lax.all_to_all(outgoing, "mp", split_axis=3, concat_axis=2, tiled=True)
    gathered = lax.all_gather(returned, "dp", axis=1, tiled=True)
    flat_updates = gathered.reshape(positions, row_count, block_size)
    inverse_order = jnp.argsort(block_order)
    block_updates = flat_updates[inverse_order]
    update = block_updates.reshape(block_rows, block_cols, row_count, block_size).transpose(
        0, 2, 1, 3
    )
    update = update.reshape(block_rows, row_count, block_cols * block_size)
    return (new_statistics, new_roots, update)


def solution(mesh):
    placed = (
        P("dp", None, "mp", None),
        P(None, None, "dp", "mp", None, None),
        P(None, None, "dp", "mp", None, None),
        P(),
    )
    return jax.shard_map(
        shards,
        mesh=mesh,
        in_specs=placed,
        out_specs=(
            P(None, None, "dp", "mp", None, None),
            P(None, None, "dp", "mp", None, None),
            P(None, "mp", None),
        ),
        check_vma=False,
    )
```

profile of v0, /device:TPU:0, one launch (start us, length us, event | category | flops | bytes accessed | tf_op | source)
XLA Modules:
  0.0 1006.0 jit_solution(18044005416415737644)
XLA Ops:
  7.2 18.4 %reshape.144 = bf16[8,64,20,512]{3,2,1,0:T(8,128)(2,1)} reshape(bf16[1,8,64,10240]{3,2,1,0:T(8,128)(2,1)} %param.6) | data formatting | bytes 20971520 | tf_op jit(solution)/shard_map/reshape | solution.py:53
  25.6 11.3 %copy.38 = bf16[8,64,20,512]{3,1,2,0:T(8,128)(2,1)} copy(bf16[8,64,20,512]{3,2,1,0:T(8,128)(2,1)} %reshape.144) | data formatting | bytes 20971520 | tf_op jit(solution)/shard_map/reshape | solution.py:53
  38.5 12.4 %gather_fusion.1 = bf16[160,64,512]{2,1,0:T(8,128)(2,1)} fusion(bf16[8,64,20,512]{3,1,2,0:T(8,128)(2,1)} %copy.38, s32[160]{0:T(256)S(1)} %bitcast.169), kind=kCustom, calls=%fused_computation.1 | custom fusion | bytes 20972800 | tf_op jit(solution)/shard_map/gather | solution.py:54
  51.0 9.9 broadcast_select_fusion
  60.9 9.7 copy.39
  70.6 123.3 %all_to_all.24 = bf16[5,4,8,64,512]{4,3,1,0,2:T(8,128)(2,1)} all-to-all(bf16[5,4,8,64,512]{4,3,1,0,2:T(8,128)(2,1)} %copy.39), channel_id=1, replica_groups=mesh['dp'=4,'mp'=8] {'mp'}, dimensions={2} | all-to-all | bytes 20971520 | tf_op jit(solution)/shard_map/all_to_all | solution.py:57
  193.9 9.7 copy.40
  204.9 5.6 slice_bitcast_fusion.2
  210.4 9.4 slice_bitcast_fusion
  219.9 342.5 %all-reduce.3.cloned.1.call-done = bf16[5,4,1,512,512]{4,3,1,0,2:T(8,128)(2,1)} async-done(((bf16[5,4,1,512,512]{4,3,1,0,2:T(8,128)(2,1)}), bf16[5,4,1,512,512]{4,3,1,0,2:T(8,128)(2,1)}) %all-reduce.3.cloned.1.call-update) | async-done | bytes 10485776
  562.4 4.1 dynamic-slice_bitcast_fusion
  566.5 3.0 broadcast.189
  569.6 3.0 broadcast.189.clone
  572.6 165.5 %while.19 = (s32[]{:T(128)}, f32[5,512,512]{2,1,0:T(8,128)}, f32[5,512,512]{2,1,0:T(8,128)}, bf16[5,512,512]{2,1,0:T(8,128)(2,1)}, bf16[5,512,512]{2,1,0:T(8,128...) while((s32[]{:T(128)}, f32[5,512,512]{2,1,0:T(8,128)}, ...), condition=%wide.region_4.5_spmd.clone, body=%wide.region_1.4_spmd.sunk.clone | while | flops 17192452096 | bytes 35656916 | solution.py:62
  572.9 3.0 bitcast_dynamic-update-slice_fusion.7
  585.3 2.6 fusion.171
  588.0 3.0 bitcast_dynamic-update-slice_fusion.6
  600.4 2.7 fusion.166
  603.1 2.9 fusion.172
  605.9 3.0 bitcast_dynamic-update-slice_fusion.7
  618.3 2.6 fusion.171
  621.0 3.0 bitcast_dynamic-update-slice_fusion.6
  636.0 2.9 fusion.172
  638.9 3.0 bitcast_dynamic-update-slice_fusion.7
  651.3 2.7 fusion.171
  654.0 3.0 bitcast_dynamic-update-slice_fusion.6
  666.3 2.7 fusion.166
  669.0 2.9 fusion.172
  671.9 3.0 bitcast_dynamic-update-slice_fusion.7
  684.3 2.7 fusion.171
  687.0 3.0 bitcast_dynamic-update-slice_fusion.6
  699.4 2.7 fusion.166
  702.1 2.8 fusion.172
  704.9 3.0 bitcast_dynamic-update-slice_fusion.7
  717.3 2.6 fusion.171
  720.0 3.0 bitcast_dynamic-update-slice_fusion.6
  732.3 2.7 fusion.166
  735.1 2.9 fusion.172
  738.1 3.4 copy.51
  741.5 52.5 %all_to_all.25 = bf16[5,1,1,512,512]{4,0,2,1,3:T(8,128)(2,1)S(1)} all-to-all(bf16[5,1,1,512,512]{4,0,2,1,3:T(8,128)(2,1)S(1)} %bitcast.164), channel_id=1, replica_groups=mesh['dp'=4,'mp'=8] {'mp'}, dimensions={3} | all-to-all | bytes 5242880 | tf_op jit(solution)/shard_map/all_to_all | solution.py:79
  796.6 3.2 sort.17
  799.8 2.8 select_bitcast_fusion.3
  802.6 2.8 maximum_bitcast_fusion.1
  805.4 7.1 select_bitcast_fusion.1
  812.5 6.4 maximum_bitcast_fusion
  818.9 158.9 %all-gather.2.cloned.1.call-done = bf16[5,4,8,64,512]{4,3,2,1,0:T(8,128)(2,1)} async-done(((bf16[5,1,8,64,512]{4,3,2,1,0:T(8,128)(2,1)}), bf16[5,4,8,64,512]{4,3,2,1,0:T(8,128)(2,1)}) %all-gather.2.cloned.1.call-update) | async-done | bytes 10485776 | tf_op jit(solution)/shard_map/all_gather | solution.py:80
  977.8 11.5 %gather_fusion.2 = bf16[160,64,512]{2,1,0:T(8,128)(2,1)} fusion(bf16[160,64,512]{2,1,0:T(8,128)(2,1)} %bitcast.168, s32[1024]{0:T(1024)S(1)} %pad_clamp_fusion), kind=kCustom, calls=%fused_computation.2 | custom fusion | bytes 20972160 | tf_op jit(solution)/shard_map/gather | solution.py:83
  989.3 9.6 copy.49
  (75 shorter events, 93.5 us)
Async XLA Ops:
  7.2 555.2 %all-reduce.3.cloned.1.call-start = ((), (), s32[]{:S(2)}) async-start(), calls=%async_computation.3 | async-start | bytes 20971520
  25.6 11.3 %copy-start = (s32[160]{0:T(256)S(1)}, s32[160]{0:T(256)}, u32[]{:S(2)}) copy-start(s32[160]{0:T(256)} %param.9) | copy-start | bytes 1924
  203.6 0.7 copy-start.2
  203.7 774.2 %all-gather.2.cloned.1.call-start = ((), (), s32[]{:S(2)}) async-start(), calls=%async_computation.2 | async-start | bytes 13107200 | tf_op jit(solution)/shard_map/all_gather | solution.py:80
  794.0 5.7 copy-start.1
Sparse Core Ops, SparseCore 0:
  203.8 358.5 all-reduce.2
  796.7 181.0 all-gather.1
where the time goes:
time: 1020 us; the launch traced here: 1010 us
  waiting for transfers between devices  501 us (49%)
  blocking collectives  176 us (17%)
  matrix products  147 us (14%)
  local copies, waits for them, and re-layouts  116 us (11%)
  other arithmetic  41.7 us (4%)
  between operations  14.3 us (1%)
    unnamed x3, waiting for transfers between devices  343 us
    all_gather x1, waiting for transfers between devices, shards(): gathered = lax.all_gather(returned, 'dp', axis=1, tiled=True)  159 us
    all_to_all x1, blocking collectives, shards(): lax.all_to_all(pieces, 'mp', split_axis=2, concat_axis=3, tiled=True)  123 us
    all_to_all x1, blocking collectives, shards(): lax.all_to_all(outgoing, 'mp', split_axis=3, concat_axis=2, tiled=True)  52.5 us
    dot_general x20, matrix products, inverse_root(): iterate = jnp.dot(iterate, factor, precision=lax.Precision.HIGHEST)  45.7 us
    reshape x2, local copies, waits for them, and re-layouts, shards(): grad_parts.reshape(block_rows, row_count, block_cols, block_size)  29.6 us
  transfers between devices with their start and end apart: 2, of which 2 were waited for; matrix products, arithmetic and copies ran while one was open for 4% of the time, Pallas kernels for 0%

commit v1 on v0

v1 whole, which is shorter than its diff:
```python
import functools

import jax
import jax.numpy as jnp
from jax import lax
from jax.experimental import pallas as pl
from jax.experimental.pallas import tpu as pltpu
from jax.sharding import PartitionSpec as P

DECAY = 0.95
MESH = pl.DeviceIdType.MESH
COEFS = (
    25.0 / 16.0,
    -5.0 / 16.0 - 3125.0 / 4096.0,
    3125.0 / 4096.0,
    -1250.0 / 4096.0,
    250.0 / 4096.0,
    -25.0 / 4096.0,
    1.0 / 4096.0,
)


def gather_kernel(order_ref, grad_ref, out_ref, sem):
    count, _, width = out_ref.shape
    per_row = grad_ref.shape[3] // width

    def issue(j, carry):
        block = order_ref[j]
        column = pl.multiple_of((block % per_row) * width, width)
        pltpu.make_async_copy(
            grad_ref.at[0, block // per_row, :, pl.ds(column, width)], out_ref.at[j], sem
        ).start()
        return carry

    lax.fori_loop(0, count, issue, 0)
    pltpu.make_async_copy(out_ref, out_ref, sem).wait()


def scatter_kernel(order_ref, tiles_ref, out_ref, sem):
    count = order_ref.shape[0]
    width = tiles_ref.shape[2]
    per_row = out_ref.shape[2] // width

    def issue(j, carry):
        block = order_ref[j]
        column = pl.multiple_of((block % per_row) * width, width)
        pltpu.make_async_copy(
            tiles_ref.at[j], out_ref.at[block // per_row, :, pl.ds(column, width)], sem
        ).start()
        return carry

    lax.fori_loop(0, count, issue, 0)
    pltpu.make_async_copy(out_ref, out_ref, sem).wait()


def dot(a, b, dims=((1,), (0,))):
    return lax.dot_general(a, b, (dims, ((), ())), preferred_element_type=jnp.float32)


def inverse_root(matrix):
    magnitude = jnp.sqrt(jnp.sum(matrix * matrix, keepdims=True)) + 1e-06
    m1 = matrix * (1.0 / magnitude)
    scale = lax.rsqrt(jnp.sqrt(magnitude))
    h1 = m1.astype(jnp.bfloat16)
    m2 = dot(h1, h1)
    m3 = dot(h1, m2.astype(jnp.bfloat16))
    high = COEFS[4] * m1 + COEFS[5] * m2 + COEFS[6] * m3
    top = dot(m3.astype(jnp.bfloat16), high.astype(jnp.bfloat16))
    size = matrix.shape[0]
    diagonal = lax.broadcasted_iota(jnp.int32, (size, size), 0) == lax.broadcasted_iota(
        jnp.int32, (size, size), 1
    )
    total = top + COEFS[1] * m1 + COEFS[2] * m2 + COEFS[3] * m3
    total = total + jnp.where(diagonal, COEFS[0], 0.0)
    return total * scale


def step_kernel(
    slots, dn, mn, block_count,
    pieces, stats_in, roots_in,
    stats_out, roots_out, gathered,
    recv, summed, grads, upd, stats, roots,
    rs_send, rs_recv, a1_send, a1_recv, a2_send, a2_recv, ag_send, ag_recv,
    in_sem, out_sem,
):
    d = lax.axis_index("dp")
    m = lax.axis_index("mp")
    rows = grads.shape[1] // mn

    barrier = pltpu.get_barrier_semaphore()

    def greet(k, carry):
        pl.semaphore_signal(barrier, inc=1, device_id=(d, lax.rem(m + k, mn)), device_id_type=MESH)
        return carry

    lax.fori_loop(1, mn, greet, 0)

    @pl.when(d > 0)
    def _():
        pl.semaphore_signal(barrier, inc=1, device_id=(d - 1, m), device_id_type=MESH)

    @pl.when(d < dn - 1)
    def _():
        pl.semaphore_signal(barrier, inc=1, device_id=(d + 1, m), device_id_type=MESH)

    def stat_in(s, side):
        return pltpu.make_async_copy(stats_in.at[side, s], stats.at[side, s], in_sem.at[s, side])

    def root_in(s, side):
        return pltpu.make_async_copy(roots_in.at[side, s], roots.at[side, s], in_sem.at[s, 2 + side])

    def stat_out(s, side):
        return pltpu.make_async_copy(stats.at[side, s], stats_out.at[side, s], out_sem.at[s, side])

    def root_out(s, side):
        return pltpu.make_async_copy(roots.at[side, s], roots_out.at[side, s], out_sem.at[s, 2 + side])

    def fetch(s, carry):
        for side in range(2):
            root_in(s, side).start()
            stat_in(s, side).start()
        return carry

    lax.fori_loop(0, slots, fetch, 0)

    ends = (d == 0).astype(jnp.int32) + (d == dn - 1).astype(jnp.int32)
    pl.semaphore_wait(barrier, mn + 1 - ends)

    def rs_copy(s, o, step, first):
        place = o + 1 if step > 0 else o
        return pltpu.make_async_remote_copy(
            src_ref=pieces.at[s, o] if first else recv.at[s, place],
            dst_ref=recv.at[s, place],
            send_sem=rs_send.at[s, place],
            recv_sem=rs_recv.at[s, place],
            device_id=(d + step, m),
            device_id_type=MESH,
        )

    def ag_copy(s, o, step):
        return pltpu.make_async_remote_copy(
            src_ref=gathered.at[s, o],
            dst_ref=gathered.at[s, o],
            send_sem=ag_send.at[s, o, 1 if step > 0 else 0],
            recv_sem=ag_recv.at[s, o],
            device_id=(d + step, m),
            device_id_type=MESH,
        )

    def rows_of(k):
        return pl.ds(pl.multiple_of(k * rows, rows), rows)

    def a1_copy(s, k):
        return pltpu.make_async_remote_copy(
            src_ref=summed.at[s, rows_of(k)],
            dst_ref=grads.at[s, rows_of(m)],
            send_sem=a1_send.at[s, k],
            recv_sem=a1_recv.at[s, m],
            device_id=(d, k),
            device_id_type=MESH,
        )

    def a2_copy(s, k):
        return pltpu.make_async_remote_copy(
            src_ref=upd.at[s, rows_of(k)],
            dst_ref=gathered.at[s, d, rows_of(m)],
            send_sem=a2_send.at[s, k],
            recv_sem=a2_recv.at[s, m],
            device_id=(d, k),
            device_id_type=MESH,
        )

    def a1_arrival(s, k):
        return pltpu.make_async_copy(grads.at[s, rows_of(k)], grads.at[s, rows_of(k)], a1_recv.at[s, k])

    def a2_arrival(s, k):
        return pltpu.make_async_copy(
            gathered.at[s, d, rows_of(k)], gathered.at[s, d, rows_of(k)], a2_recv.at[s, k]
        )

    def peers(action):
        def body(k, carry):
            action(lax.rem(m + k, mn))
            return carry

        lax.fori_loop(1, mn, body, 0)

    def add_pieces(s, o, place):
        recv[s, place] = (
            recv[s, place].astype(jnp.float32) + pieces[s, o].astype(jnp.float32)
        ).astype(jnp.bfloat16)

    def rs_start(s):
        @pl.when(d == 0)
        def _():
            for o in range(dn - 1, 0, -1):
                rs_copy(s, o, 1, True).start()

        @pl.when(d == dn - 1)
        def _():
            for o in range(dn - 1):
                rs_copy(s, o, -1, True).start()

    def relay(s, rank):
        right, left = dn - 1 - rank, rank

        @pl.when((s < slots) & (d > 0) & (d < right))
        def _():
            rs_copy(s, right, 1, False).wait_recv()
            add_pieces(s, right, right + 1)
            rs_copy(s, right, 1, False).start()

        @pl.when((s < slots) & (d < dn - 1) & (d > left))
        def _():
            rs_copy(s, left, -1, False).wait_recv()
            add_pieces(s, left, left)
            rs_copy(s, left, -1, False).start()

        near_left, near_right = d - 1 - rank, d + 1 + rank

        @pl.when((s > 0) & (d < dn - 1) & (near_left >= 0))
        def _():
            ag_copy(s - 1, near_left, 1).wait_recv()
            ag_copy(s - 1, near_left, 1).start()

        @pl.when((s > 0) & (d > 0) & (near_right < dn))
        def _():
            ag_copy(s - 1, near_right, -1).wait_recv()
            ag_copy(s - 1, near_right, -1).start()

    def own(s):
        @pl.when(d > 0)
        def _():
            rs_copy(s, d, 1, False).wait_recv()

        @pl.when(d < dn - 1)
        def _():
            rs_copy(s, d, -1, False).wait_recv()

        @pl.when(d == 0)
        def _():
            summed[s] = (
                recv[s, d].astype(jnp.float32) + pieces[s, d].astype(jnp.float32)
            ).astype(jnp.bfloat16)

        @pl.when(d == dn - 1)
        def _():
            summed[s] = (
                recv[s, d + 1].astype(jnp.float32) + pieces[s, d].astype(jnp.float32)
            ).astype(jnp.bfloat16)

        @pl.when((d > 0) & (d < dn - 1))
        def _():
            summed[s] = (
                recv[s, d].astype(jnp.float32)
                + recv[s, d + 1].astype(jnp.float32)
                + pieces[s, d].astype(jnp.float32)
            ).astype(jnp.bfloat16)

        peers(lambda k: a1_copy(s, k).start())
        grads[s, rows_of(m)] = summed[s, rows_of(m)]
        for side in range(2):
            root_in(s, side).wait()
        peers(lambda k: a1_arrival(s, k).wait())
        scaled = dot(roots[0, s], grads[s]).astype(jnp.bfloat16)
        upd[s] = dot(scaled, roots[1, s]).astype(jnp.bfloat16)
        peers(lambda k: a2_copy(s, k).start())
        mine = pltpu.make_async_copy(
            upd.at[s, rows_of(m)], gathered.at[s, d, rows_of(m)], a2_send.at[s, m]
        )
        mine.start()
        mine.wait()
        peers(lambda k: a2_arrival(s, k).wait())

        @pl.when(d < dn - 1)
        def _():
            ag_copy(s, d, 1).start()

        @pl.when(d > 0)
        def _():
            ag_copy(s, d, -1).start()

    def statistic(s, side):
        live = (s * dn + d) * mn + m < block_count
        stat_in(s, side).wait()
        block = grads[s]
        gram = dot(block, block, ((1 - side,), (1 - side,)))
        new = DECAY * stats[side, s] + (1.0 - DECAY) * gram
        stats[side, s] = jnp.where(live, new, 0.0)
        root = inverse_root(new)
        roots[side, s] = jnp.where(live, root, 0.0).astype(jnp.bfloat16)
        stat_out(s, side).start()
        root_out(s, side).start()

    rs_start(0)

    def step(s, carry):
        @pl.when(s + 1 < slots)
        def _():
            rs_start(s + 1)

        for rank in range(dn - 1):
            relay(s, rank)

        @pl.when(s < slots)
        def _():
            own(s)
            for side in range(2):
                statistic(s, side)

        return carry

    lax.fori_loop(0, slots + 1, step, 0)

    def finish(s, carry):
        for side in range(2):
            stat_out(s, side).wait()
            root_out(s, side).wait()
        peers(lambda k: a1_copy(s, k).wait_send())
        peers(lambda k: a2_copy(s, k).wait_send())
        for o in range(dn):
            @pl.when(o > d)
            def _():
                rs_copy(s, o, 1, False).wait_send()

            @pl.when(o < d)
            def _():
                rs_copy(s, o, -1, False).wait_send()

            @pl.when((o <= d) & (d < dn - 1))
            def _():
                ag_copy(s, o, 1).wait_send()

            @pl.when((o >= d) & (d > 0))
            def _():
                ag_copy(s, o, -1).wait_send()

            @pl.when((o < d) & (d == dn - 1))
            def _():
                ag_copy(s, o, 1).wait_recv()

            @pl.when((o > d) & (d == 0))
            def _():
                ag_copy(s, o, -1).wait_recv()

        return carry

    lax.fori_loop(0, slots, finish, 0)


def shards(grad_parts, statistics, prior_roots, block_order):
    dn = lax.axis_size("dp")
    mn = lax.axis_size("mp")
    width = statistics.shape[-1]
    slots = statistics.shape[1]
    rows = grad_parts.shape[2]
    block_count = block_order.shape[0]
    positions = slots * dn * mn
    chosen = block_order
    if positions > block_count:
        chosen = jnp.pad(block_order, (0, positions - block_count))
    anywhere = pl.BlockSpec(memory_space=pl.ANY)
    indices = pl.BlockSpec(memory_space=pltpu.SMEM)
    tile_bytes = positions * rows * width * 2
    pieces = pl.pallas_call(
        gather_kernel,
        out_shape=jax.ShapeDtypeStruct((positions, rows, width), jnp.bfloat16),
        in_specs=[indices, anywhere],
        out_specs=anywhere,
        scratch_shapes=[pltpu.SemaphoreType.DMA],
        cost_estimate=pl.CostEstimate(flops=0, bytes_accessed=2 * tile_bytes, transcendentals=0),
    )(chosen, grad_parts)
    pieces = pieces.reshape(slots, dn, width, width)
    dma = pltpu.SemaphoreType.DMA
    block = (width, width)
    new_stats, new_roots, gathered = pl.pallas_call(
        functools.partial(step_kernel, slots, dn, mn, block_count),
        out_shape=(
            jax.ShapeDtypeStruct((2, slots) + block, jnp.float32),
            jax.ShapeDtypeStruct((2, slots) + block, jnp.bfloat16),
            jax.ShapeDtypeStruct((slots, dn) + block, jnp.bfloat16),
        ),
        in_specs=[pl.BlockSpec(memory_space=pltpu.VMEM), anywhere, anywhere],
        out_specs=(anywhere, anywhere, anywhere),
        scratch_shapes=[
            pltpu.VMEM((slots, dn + 1) + block, jnp.bfloat16),
            pltpu.VMEM((slots,) + block, jnp.bfloat16),
            pltpu.VMEM((slots,) + block, jnp.bfloat16),
            pltpu.VMEM((slots,) + block, jnp.bfloat16),
            pltpu.VMEM((2, slots) + block, jnp.float32),
            pltpu.VMEM((2, slots) + block, jnp.bfloat16),
            dma((slots, dn + 1)),
            dma((slots, dn + 1)),
            dma((slots, mn)),
            dma((slots, mn)),
            dma((slots, mn)),
            dma((slots, mn)),
            dma((slots, dn, 2)),
            dma((slots, dn)),
            dma((slots, 4)),
            dma((slots, 4)),
        ],
        compiler_params=pltpu.CompilerParams(
            collective_id=0, has_side_effects=True, vmem_limit_bytes=60 * 1024 * 1024
        ),
        cost_estimate=pl.CostEstimate(
            flops=slots * 20 * width**3, bytes_accessed=10 * tile_bytes, transcendentals=0
        ),
    )(
        pieces,
        statistics.reshape((2, slots) + block),
        prior_roots.reshape((2, slots) + block),
    )
    update = pl.pallas_call(
        scatter_kernel,
        out_shape=jax.ShapeDtypeStruct(grad_parts.shape[1:], jnp.bfloat16),
        in_specs=[indices, anywhere],
        out_specs=anywhere,
        scratch_shapes=[pltpu.SemaphoreType.DMA],
        cost_estimate=pl.CostEstimate(flops=0, bytes_accessed=2 * tile_bytes, transcendentals=0),
    )(block_order, gathered.reshape(positions, rows, width))
    return (
        new_stats.reshape(statistics.shape),
        new_roots.reshape(prior_roots.shape),
        update,
    )


def solution(mesh):
    placed = (
        P("dp", None, "mp", None),
        P(None, None, "dp", "mp", None, None),
        P(None, None, "dp", "mp", None, None),
        P(),
    )
    return jax.shard_map(
        shards,
        mesh=mesh,
        in_specs=placed,
        out_specs=(
            P(None, None, "dp", "mp", None, None),
            P(None, None, "dp", "mp", None, None),
            P(None, "mp", None),
        ),
        check_vma=False,
    )
```

time: 1020 us -> 1070 us (1.049); the launches traced: 1010 us -> 1070 us
  Pallas kernels: 0 us -> 1060 us
  waiting for transfers between devices: 501 us -> 0 us
  blocking collectives: 176 us -> 0 us
  matrix products: 147 us -> 0 us
  local copies, waits for them, and re-layouts: 116 us -> 11.9 us
  other arithmetic: 41.7 us -> 0 us
  between operations: 14.3 us -> 0.66 us
    pallas_call x0 -> x3, Pallas kernels: none -> 1060 us  [the longest x1 417 us: shards(): pl.pallas_call(functools.partial(step_kernel, slots, dn, mn, block_count)...]
    unnamed x3 -> x0, waiting for transfers between devices: 343 us -> none
    all_to_all x2 -> x0, blocking collectives: 176 us -> none  [the longest x1 123 us: shards(): lax.all_to_all(pieces, 'mp', split_axis=2, concat_axis=3, tiled=True)]
    all_gather x1 -> x0, waiting for transfers between devices: 159 us -> none  [shards(): gathered = lax.all_gather(returned, 'dp', axis=1, tiled=True)]
    dot_general x65 -> x0, matrix products: 147 us -> none  [the longest x20 45.7 us: inverse_root(): iterate = jnp.dot(iterate, factor, precision=lax.Precision.HIGHEST)]
    reshape x4 -> x0, local copies, waits for them, and re-layouts: 43.4 us -> none  [the longest x2 29.6 us: shards(): grad_parts.reshape(block_rows, row_count, block_cols, block_size)]
    gather x3 -> x0, local copies, waits for them, and re-layouts: 25.5 us -> none  [the longest x1 12.4 us: shards(): pieces = grad_tiles[chosen // block_cols, :, chosen % block_cols, :]]
    squeeze x2 -> x0, local copies, waits for them, and re-layouts: 15 us -> none  [the longest x1 9.42 us: shards(): stats_local[1]]
  transfers between devices with their start and end apart: 2 -> 0, of which waited for: 2 -> 0; matrix products, arithmetic and copies ran while one was open for 4% -> 0% of each run, Pallas kernels for 0% -> 0%
where the time goes in v1:
time: 1070 us
  Pallas kernels  1060 us (99%)
  local copies, waits for them, and re-layouts  11.9 us (1%)
    pallas_call x1, Pallas kernels, shards(): pl.pallas_call(functools.partial(step_kernel, slots, dn, mn, block_count)...  417 us
    pallas_call x1, Pallas kernels, shards(): pl.pallas_call(scatter_kernel, out_shape=jax.ShapeDtypeStruct(grad_parts....  319 us
    pallas_call x1, Pallas kernels, shards(): pl.pallas_call(gather_kernel, out_shape=jax.ShapeDtypeStruct((positions,...  319 us

profile of v1, /device:TPU:0, one launch (start us, length us, event | category | flops | bytes accessed | tf_op | source)
XLA Modules:
  0.0 1068.6 jit_solution(2400885585862778996)
XLA Ops:
  0.6 319.5 %shard_map.67 = bf16[160,64,512]{2,1,0:T(8,128)(2,1)} custom-call(s32[160]{0:T(256)} %order_ref.3, bf16[1,8,64,10240]{3,2,1,0:T(8,128)(2,1)} %grad_ref.1), custom_call_target="tpu_custom_call" | custom-call | bytes 20971520 | tf_op jit(solution)/shard_map/pallas_call | solution.py:365
  320.1 417.1 %shard_map.68 = (f32[2,5,512,512]{3,2,1,0:T(8,128)}, bf16[2,5,512,512]{3,2,1,0:T(8,128)(2,1)}, bf16[5,4,512,512]{3,2,1,0:T(8,128)(2,1)}) custom-call(bf16[5,4,512,512]{3,2,1,0:T(8,128)(2,1)} %bitcast.12, f32[2,5,512,512]{3,2,1,0:T(8,128)} %bitcast.14, bf16[2,5,512,512]{3,2,1,0:T(8,128)(2,1)} %bitcast.15), custom_call_target="tpu_custom_call" | custom-call | flops 13421772800 | bytes 104857600 | tf_op jit(solution)/shard_map/pallas_call | solution.py:376
  737.2 319.5 %shard_map.69 = bf16[8,64,10240]{2,1,0:T(8,128)(2,1)} custom-call(s32[160]{0:T(256)} %order_ref.3, bf16[160,64,512]{2,1,0:T(8,128)(2,1)} %bitcast.11), custom_call_target="tpu_custom_call" | custom-call | bytes 20971520 | tf_op jit(solution)/shard_map/pallas_call | solution.py:414
  1056.7 0.0 copy-start
  1056.7 9.5 copy.11
  1066.2 0.0 copy-done
  1066.2 2.4 copy.12
Async XLA Ops:
  1056.7 9.5 copy-start

commit v2 on v1

--- a/solution.py
+++ b/solution.py
@@ -18,22 +18,6 @@
     -25.0 / 4096.0,
     1.0 / 4096.0,
 )
-
-
-def gather_kernel(order_ref, grad_ref, out_ref, sem):
-    count, _, width = out_ref.shape
-    per_row = grad_ref.shape[3] // width
-
-    def issue(j, carry):
-        block = order_ref[j]
-        column = pl.multiple_of((block % per_row) * width, width)
-        pltpu.make_async_copy(
-            grad_ref.at[0, block // per_row, :, pl.ds(column, width)], out_ref.at[j], sem
-        ).start()
-        return carry
-
-    lax.fori_loop(0, count, issue, 0)
-    pltpu.make_async_copy(out_ref, out_ref, sem).wait()
 
 
 def scatter_kernel(order_ref, tiles_ref, out_ref, sem):
@@ -77,15 +61,26 @@
 
 def step_kernel(
     slots, dn, mn, block_count,
-    pieces, stats_in, roots_in,
-    stats_out, roots_out, gathered,
-    recv, summed, grads, upd, stats, roots,
+    order, grad_in, stats_in, roots_in,
+    stats_out, roots_out, gathered_out,
+    parts, recv, gathered, grads, stats, roots,
     rs_send, rs_recv, a1_send, a1_recv, a2_send, a2_recv, ag_send, ag_recv,
-    in_sem, out_sem,
+    in_sem, out_sem, part_sem, tile_sem,
 ):
     d = lax.axis_index("dp")
     m = lax.axis_index("mp")
     rows = grads.shape[1] // mn
+    width = grads.shape[2]
+    per_row = grad_in.shape[3] // width
+
+    def pick(block, carry):
+        column = pl.multiple_of((block % per_row) * width, width)
+        pltpu.make_async_copy(
+            grad_in.at[0, block // per_row, :, pl.ds(column, width)], parts.at[block], part_sem
+        ).start()
+        return carry
+
+    lax.fori_loop(0, parts.shape[0], pick, 0)
 
     barrier = pltpu.get_barrier_semaphore()
 
@@ -126,10 +121,12 @@
     ends = (d == 0).astype(jnp.int32) + (d == dn - 1).astype(jnp.int32)
     pl.semaphore_wait(barrier, mn + 1 - ends)
 
-    def rs_copy(s, o, step, first):
+    pltpu.make_async_copy(parts, parts, part_sem).wait()
+
+    def rs_copy(s, o, step):
         place = o + 1 if step > 0 else o
         return pltpu.make_async_remote_copy(
-            src_ref=pieces.at[s, o] if first else recv.at[s, place],
+            src_ref=recv.at[s, place],
             dst_ref=recv.at[s, place],
             send_sem=rs_send.at[s, place],
             recv_sem=rs_recv.at[s, place],
@@ -152,7 +149,7 @@
 
     def a1_copy(s, k):
         return pltpu.make_async_remote_copy(
-            src_ref=summed.at[s, rows_of(k)],
+            src_ref=recv.at[s, d, rows_of(k)],
             dst_ref=grads.at[s, rows_of(m)],
             send_sem=a1_send.at[s, k],
             recv_sem=a1_recv.at[s, m],
@@ -162,7 +159,7 @@
 
     def a2_copy(s, k):
         return pltpu.make_async_remote_copy(
-            src_ref=upd.at[s, rows_of(k)],
+            src_ref=recv.at[s, d + 1, rows_of(k)],
             dst_ref=gathered.at[s, d, rows_of(m)],
             send_sem=a2_send.at[s, k],
             recv_sem=a2_recv.at[s, m],
@@ -185,36 +182,57 @@
 
         lax.fori_loop(1, mn, body, 0)
 
-    def add_pieces(s, o, place):
-        recv[s, place] = (
-            recv[s, place].astype(jnp.float32) + pieces[s, o].astype(jnp.float32)
-        ).astype(jnp.bfloat16)
-
-    def rs_start(s):
-        @pl.when(d == 0)
-        def _():
-            for o in range(dn - 1, 0, -1):
-                rs_copy(s, o, 1, True).start()
-
-        @pl.when(d == dn - 1)
-        def _():
-            for o in range(dn - 1):
-                rs_copy(s, o, -1, True).start()
+    def add_pieces(s, o, target, *terms):
+        def body(p, carry):
+            piece = parts[order[(s * dn + o) * mn + p]]
+            at = rows_of(p)
+            if terms:
+                total = piece.astype(jnp.float32)
+                for t in terms:
+                    total = total + recv[s, t, at].astype(jnp.float32)
+                piece = total.astype(jnp.bfloat16)
+            recv[s, target, at] = piece
+            return carry
+
+        lax.fori_loop(0, mn, body, 0)
+
+    def rs_start(s, rank):
+        right, left = dn - 1 - rank, rank
+
+        @pl.when((s < slots) & (d == 0))
+        def _():
+            add_pieces(s, right, right + 1)
+
+            @pl.when(s > 0)
+            def _():
+                rs_copy(s - 1, right, 1).wait_send()
+
+            rs_copy(s, right, 1).start()
+
+        @pl.when((s < slots) & (d == dn - 1))
+        def _():
+            add_pieces(s, left, left)
+
+            @pl.when(s > 0)
+            def _():
+                rs_copy(s - 1, left, -1).wait_send()
+
+            rs_copy(s, left, -1).start()
 
     def relay(s, rank):
         right, left = dn - 1 - rank, rank
 
         @pl.when((s < slots) & (d > 0) & (d < right))
         def _():
-            rs_copy(s, right, 1, False).wait_recv()
-            add_pieces(s, right, right + 1)
-            rs_copy(s, right, 1, False).start()
+            rs_copy(s, right, 1).wait_recv()
+            add_pieces(s, right, right + 1, right + 1)
+            rs_copy(s, right, 1).start()
 
         @pl.when((s < slots) & (d < dn - 1) & (d > left))
         def _():
-            rs_copy(s, left, -1, False).wait_recv()
-            add_pieces(s, left, left)
-            rs_copy(s, left, -1, False).start()
+            rs_copy(s, left, -1).wait_recv()
+            add_pieces(s, left, left, left)
+            rs_copy(s, left, -1).start()
 
         near_left, near_right = d - 1 - rank, d + 1 + rank
 
@@ -231,45 +249,33 @@
     def own(s):
         @pl.when(d > 0)
         def _():
-            rs_copy(s, d, 1, False).wait_recv()
+            rs_copy(s, d, 1).wait_recv()
 
         @pl.when(d < dn - 1)
         def _():
-            rs_copy(s, d, -1, False).wait_recv()
+            rs_copy(s, d, -1).wait_recv()
 
         @pl.when(d == 0)
         def _():
-            summed[s] = (
-                recv[s, d].astype(jnp.float32) + pieces[s, d].astype(jnp.float32)
-            ).astype(jnp.bfloat16)
+            add_pieces(s, d, d, d)
 
         @pl.when(d == dn - 1)
         def _():
-            summed[s] = (
-                recv[s, d + 1].astype(jnp.float32) + pieces[s, d].astype(jnp.float32)
-            ).astype(jnp.bfloat16)
+            add_pieces(s, d, d, d + 1)
 
         @pl.when((d > 0) & (d < dn - 1))
         def _():
-            summed[s] = (
-                recv[s, d].astype(jnp.float32)
-                + recv[s, d + 1].astype(jnp.float32)
-                + pieces[s, d].astype(jnp.float32)
-            ).astype(jnp.bfloat16)
+            add_pieces(s, d, d, d, d + 1)
 
         peers(lambda k: a1_copy(s, k).start())
-        grads[s, rows_of(m)] = summed[s, rows_of(m)]
+        grads[s, rows_of(m)] = recv[s, d, rows_of(m)]
         for side in range(2):
             root_in(s, side).wait()
         peers(lambda k: a1_arrival(s, k).wait())
         scaled = dot(roots[0, s], grads[s]).astype(jnp.bfloat16)
-        upd[s] = dot(scaled, roots[1, s]).astype(jnp.bfloat16)
+        recv[s, d + 1] = dot(scaled, roots[1, s]).astype(jnp.bfloat16)
         peers(lambda k: a2_copy(s, k).start())
-        mine = pltpu.make_async_copy(
-            upd.at[s, rows_of(m)], gathered.at[s, d, rows_of(m)], a2_send.at[s, m]
-        )
-        mine.start()
-        mine.wait()
+        gathered[s, d, rows_of(m)] = recv[s, d + 1, rows_of(m)]
         peers(lambda k: a2_arrival(s, k).wait())
 
         @pl.when(d < dn - 1)
@@ -292,40 +298,53 @@
         stat_out(s, side).start()
         root_out(s, side).start()
 
-    rs_start(0)
+    for rank in range(dn - 1):
+        rs_start(0, rank)
 
     def step(s, carry):
-        @pl.when(s + 1 < slots)
-        def _():
-            rs_start(s + 1)
-
         for rank in range(dn - 1):
+            rs_start(s + 1, rank)
             relay(s, rank)
+            if rank < 2:
+                @pl.when(s > 0)
+                def _():
+                    statistic(s - 1, rank)
 
         @pl.when(s < slots)
         def _():
             own(s)
-            for side in range(2):
-                statistic(s, side)
 
         return carry
 
     lax.fori_loop(0, slots + 1, step, 0)
 
+    def tile_out(s):
+        return pltpu.make_async_copy(gathered.at[s], gathered_out.at[s], tile_sem.at[s])
+
     def finish(s, carry):
+        for o in range(dn):
+            @pl.when((o < d) & (d == dn - 1))
+            def _():
+                ag_copy(s, o, 1).wait_recv()
+
+            @pl.when((o > d) & (d == 0))
+            def _():
+                ag_copy(s, o, -1).wait_recv()
+
+        tile_out(s).start()
         for side in range(2):
             stat_out(s, side).wait()
             root_out(s, side).wait()
         peers(lambda k: a1_copy(s, k).wait_send())
         peers(lambda k: a2_copy(s, k).wait_send())
         for o in range(dn):
-            @pl.when(o > d)
-            def _():
-                rs_copy(s, o, 1, False).wait_send()
-
-            @pl.when(o < d)
-            def _():
-                rs_copy(s, o, -1, False).wait_send()
+            @pl.when((o > d) & ((d > 0) | (s == slots - 1)))
+            def _():
+                rs_copy(s, o, 1).wait_send()
+
+            @pl.when((o < d) & ((d < dn - 1) | (s == slots - 1)))
+            def _():
+                rs_copy(s, o, -1).wait_send()
 
             @pl.when((o <= d) & (d < dn - 1))
             def _():
@@ -335,17 +354,15 @@
             def _():
                 ag_copy(s, o, -1).wait_send()
 
-            @pl.when((o < d) & (d == dn - 1))
-            def _():
-                ag_copy(s, o, 1).wait_recv()
-
-            @pl.when((o > d) & (d == 0))
-            def _():
-                ag_copy(s, o, -1).wait_recv()
-
         return carry
 
     lax.fori_loop(0, slots, finish, 0)
+
+    def drain(s, carry):
+        tile_out(s).wait()
+        return carry
+
+    lax.fori_loop(0, slots, drain, 0)
 
 
 def shards(grad_parts, statistics, prior_roots, block_order):
@@ -362,15 +379,6 @@
     anywhere = pl.BlockSpec(memory_space=pl.ANY)
     indices = pl.BlockSpec(memory_space=pltpu.SMEM)
     tile_bytes = positions * rows * width * 2
-    pieces = pl.pallas_call(
-        gather_kernel,
-        out_shape=jax.ShapeDtypeStruct((positions, rows, width), jnp.bfloat16),
-        in_specs=[indices, anywhere],
-        out_specs=anywhere,
-        scratch_shapes=[pltpu.SemaphoreType.DMA],
-        cost_estimate=pl.CostEstimate(flops=0, bytes_accessed=2 * tile_bytes, transcendentals=0),
-    )(chosen, grad_parts)
-    pieces = pieces.reshape(slots, dn, width, width)
     dma = pltpu.SemaphoreType.DMA
     block = (width, width)
     new_stats, new_roots, gathered = pl.pallas_call(
@@ -380,12 +388,12 @@
             jax.ShapeDtypeStruct((2, slots) + block, jnp.bfloat16),
             jax.ShapeDtypeStruct((slots, dn) + block, jnp.bfloat16),
         ),
-        in_specs=[pl.BlockSpec(memory_space=pltpu.VMEM), anywhere, anywhere],
+        in_specs=[indices, anywhere, anywhere, anywhere],
         out_specs=(anywhere, anywhere, anywhere),
         scratch_shapes=[
+            pltpu.VMEM((block_count, rows, width), jnp.bfloat16),
             pltpu.VMEM((slots, dn + 1) + block, jnp.bfloat16),
-            pltpu.VMEM((slots,) + block, jnp.bfloat16),
-            pltpu.VMEM((slots,) + block, jnp.bfloat16),
+            pltpu.VMEM((slots, dn) + block, jnp.bfloat16),
             pltpu.VMEM((slots,) + block, jnp.bfloat16),
             pltpu.VMEM((2, slots) + block, jnp.float32),
             pltpu.VMEM((2, slots) + block, jnp.bfloat16),
@@ -399,15 +407,18 @@
             dma((slots, dn)),
             dma((slots, 4)),
             dma((slots, 4)),
+            dma,
+            dma((slots,)),
         ],
         compiler_params=pltpu.CompilerParams(
-            collective_id=0, has_side_effects=True, vmem_limit_bytes=60 * 1024 * 1024
+            collective_id=0, has_side_effects=True, vmem_limit_bytes=62 * 1024 * 1024
         ),
         cost_estimate=pl.CostEstimate(
             flops=slots * 20 * width**3, bytes_accessed=10 * tile_bytes, transcendentals=0
         ),
     )(
-        pieces,
+        chosen,
+        grad_parts,
         statistics.reshape((2, slots) + block),
         prior_roots.reshape((2, slots) + block),
     )
@@ -415,8 +426,9 @@
         scatter_kernel,
         out_shape=jax.ShapeDtypeStruct(grad_parts.shape[1:], jnp.bfloat16),
         in_specs=[indices, anywhere],
-        out_specs=anywhere,
+        out_specs=pl.BlockSpec(memory_space=pltpu.VMEM),
         scratch_shapes=[pltpu.SemaphoreType.DMA],
+        compiler_params=pltpu.CompilerParams(vmem_limit_bytes=40 * 1024 * 1024),
         cost_estimate=pl.CostEstimate(flops=0, bytes_accessed=2 * tile_bytes, transcendentals=0),
     )(block_order, gathered.reshape(positions, rows, width))
     return (

time: 1070 us -> 440 us (0.41)
  Pallas kernels: 1060 us -> 426 us
    pallas_call x1 -> x0, Pallas kernels: 319 us -> none  [shards(): pl.pallas_call(gather_kernel, out_shape=jax.ShapeDtypeStruct((positions,...]
    pallas_call x1, Pallas kernels: 319 us -> 9.53 us  [shards(): pl.pallas_call(scatter_kernel, out_shape=jax.ShapeDtypeStruct(grad_parts....]
where the time goes in v2:
time: 440 us
  Pallas kernels  426 us (97%)
  local copies, waits for them, and re-layouts  13.2 us (3%)
    pallas_call x1, Pallas kernels, shards(): pl.pallas_call(functools.partial(step_kernel, slots, dn, mn, block_count)...  416 us
    unnamed x8, local copies, waits for them, and re-layouts  13.2 us
    pallas_call x1, Pallas kernels, shards(): pl.pallas_call(scatter_kernel, out_shape=jax.ShapeDtypeStruct(grad_parts....  9.53 us

profile of v2, /device:TPU:0, one launch (start us, length us, event | category | flops | bytes accessed | tf_op | source)
XLA Modules:
  0.0 439.8 jit_solution(12963169592393965411)
XLA Ops:
  0.6 0.0 copy-start.1
  0.6 416.3 %shard_map.67 = (f32[2,5,512,512]{3,2,1,0:T(8,128)}, bf16[2,5,512,512]{3,2,1,0:T(8,128)(2,1)}, bf16[5,4,512,512]{3,2,1,0:T(8,128)(2,1)}) custom-call(s32[160]{0:T(256)} %order_ref.1, bf16[1,8,64,10240]{3,2,1,0:T(8,128)(2,1)} %grad_in.1, f32[2,5,512,512]{3,2,1,0:T(8,128)} %bitcast.12, bf16[2,5,512,512]{3,2,1,0:T(8,128)(2,1)} %bitcast.13), custom_call_target="tpu_custom_call" | custom-call | flops 13421772800 | bytes 104857600 | tf_op jit(solution)/shard_map/pallas_call | solution.py:384
  417.0 0.0 copy-done.1
  417.0 0.0 copy-start
  417.0 4.0 copy-done
  421.0 0.0 copy-start.2
  421.0 9.5 %shard_map.68 = bf16[8,64,10240]{2,1,0:T(8,128)(2,1)} custom-call(s32[160]{0:T(256)S(1)} %copy-done.1, bf16[160,64,512]{2,1,0:T(8,128)(2,1)S(1)} %bitcast.9), custom_call_target="tpu_custom_call" | custom-call | bytes 20971520 | tf_op jit(solution)/shard_map/pallas_call | solution.py:425
  430.5 0.0 copy-done.2
  430.5 4.1 copy.11
  434.6 5.2 %copy.12 = bf16[2,5,1,1,512,512]{5,4,3,2,1,0:T(8,128)(2,1)} copy(bf16[2,5,1,1,512,512]{5,4,3,2,1,0:T(8,128)(2,1)} %bitcast.11) | data formatting | bytes 10485760
Async XLA Ops:
  0.6 416.3 %copy-start.1 = (s32[160]{0:T(256)S(1)}, s32[160]{0:T(256)}, u32[]{:S(2)}) copy-start(s32[160]{0:T(256)} %order_ref.1) | copy-start | bytes 1924
  417.0 4.0 copy-start
  421.0 9.5 %copy-start.2 = (f32[2,5,512,512]{3,2,1,0:T(8,128)S(1)}, f32[2,5,512,512]{3,2,1,0:T(8,128)}, u32[]{:S(2)}) copy-start(f32[2,5,512,512]{3,2,1,0:T(8,128)} %get-tuple-element.6) | copy-start | bytes 31457284

commit v3 on v2

--- a/solution.py
+++ b/solution.py
@@ -219,34 +219,36 @@
 
             rs_copy(s, left, -1).start()
 
-    def relay(s, rank):
-        right, left = dn - 1 - rank, rank
-
-        @pl.when((s < slots) & (d > 0) & (d < right))
+    def relay_right(s, rank, turn):
+        right = dn - 1 - rank
+
+        @pl.when(turn & (s < slots) & (d > 0) & (d < right))
         def _():
             rs_copy(s, right, 1).wait_recv()
             add_pieces(s, right, right + 1, right + 1)
             rs_copy(s, right, 1).start()
 
-        @pl.when((s < slots) & (d < dn - 1) & (d > left))
-        def _():
-            rs_copy(s, left, -1).wait_recv()
-            add_pieces(s, left, left, left)
-            rs_copy(s, left, -1).start()
-
+    def relay_left(s, rank, turn):
+        @pl.when(turn & (s < slots) & (d < dn - 1) & (d > rank))
+        def _():
+            rs_copy(s, rank, -1).wait_recv()
+            add_pieces(s, rank, rank, rank)
+            rs_copy(s, rank, -1).start()
+
+    def forward(s, rank):
         near_left, near_right = d - 1 - rank, d + 1 + rank
 
-        @pl.when((s > 0) & (d < dn - 1) & (near_left >= 0))
-        def _():
-            ag_copy(s - 1, near_left, 1).wait_recv()
-            ag_copy(s - 1, near_left, 1).start()
-
-        @pl.when((s > 0) & (d > 0) & (near_right < dn))
-        def _():
-            ag_copy(s - 1, near_right, -1).wait_recv()
-            ag_copy(s - 1, near_right, -1).start()
-
-    def own(s):
+        @pl.when((s >= 0) & (d < dn - 1) & (near_left >= 0))
+        def _():
+            ag_copy(s, near_left, 1).wait_recv()
+            ag_copy(s, near_left, 1).start()
+
+        @pl.when((s >= 0) & (d > 0) & (near_right < dn))
+        def _():
+            ag_copy(s, near_right, -1).wait_recv()
+            ag_copy(s, near_right, -1).start()
+
+    def own_sum(s):
         @pl.when(d > 0)
         def _():
             rs_copy(s, d, 1).wait_recv()
@@ -269,6 +271,8 @@
 
         peers(lambda k: a1_copy(s, k).start())
         grads[s, rows_of(m)] = recv[s, d, rows_of(m)]
+
+    def own_update(s):
         for side in range(2):
             root_in(s, side).wait()
         peers(lambda k: a1_arrival(s, k).wait())
@@ -276,6 +280,8 @@
         recv[s, d + 1] = dot(scaled, roots[1, s]).astype(jnp.bfloat16)
         peers(lambda k: a2_copy(s, k).start())
         gathered[s, d, rows_of(m)] = recv[s, d + 1, rows_of(m)]
+
+    def own_send(s):
         peers(lambda k: a2_arrival(s, k).wait())
 
         @pl.when(d < dn - 1)
@@ -301,19 +307,38 @@
     for rank in range(dn - 1):
         rs_start(0, rank)
 
+    low = 2 * d < dn
+
     def step(s, carry):
         for rank in range(dn - 1):
             rs_start(s + 1, rank)
-            relay(s, rank)
-            if rank < 2:
-                @pl.when(s > 0)
-                def _():
-                    statistic(s - 1, rank)
+            relay_right(s, rank, low)
+            relay_left(s, rank, jnp.logical_not(low))
+        forward(s - 1, 0)
+
+        @pl.when(s > 0)
+        def _():
+            statistic(s - 1, 0)
+
+        for rank in range(dn - 1):
+            relay_left(s, rank, low)
+            relay_right(s, rank, jnp.logical_not(low))
 
         @pl.when(s < slots)
         def _():
-            own(s)
-
+            own_sum(s)
+
+        @pl.when(s > 0)
+        def _():
+            statistic(s - 1, 1)
+
+        @pl.when(s < slots)
+        def _():
+            own_update(s)
+            own_send(s)
+
+        for rank in range(1, dn - 1):
+            forward(s - 1, rank)
         return carry
 
     lax.fori_loop(0, slots + 1, step, 0)

time: 440 us -> 351 us (0.80)
  Pallas kernels: 426 us -> 337 us
    pallas_call x1, Pallas kernels: 416 us -> 327 us  [shards(): pl.pallas_call(functools.partial(step_kernel, slots, dn, mn, block_count)...]
where the time goes in v3:
time: 351 us
  Pallas kernels  337 us (96%)
  local copies, waits for them, and re-layouts  13.2 us (4%)
    pallas_call x1, Pallas kernels, shards(): pl.pallas_call(functools.partial(step_kernel, slots, dn, mn, block_count)...  327 us
    unnamed x8, local copies, waits for them, and re-layouts  13.2 us
    pallas_call x1, Pallas kernels, shards(): pl.pallas_call(scatter_kernel, out_shape=jax.ShapeDtypeStruct(grad_parts....  9.53 us

profile of v3, /device:TPU:0, one launch (start us, length us, event | category | flops | bytes accessed | tf_op | source)
XLA Modules:
  0.0 350.7 jit_solution(14032327778087911009)
XLA Ops:
  0.6 0.0 copy-start.1
  0.6 327.2 %shard_map.67 = (f32[2,5,512,512]{3,2,1,0:T(8,128)}, bf16[2,5,512,512]{3,2,1,0:T(8,128)(2,1)}, bf16[5,4,512,512]{3,2,1,0:T(8,128)(2,1)}) custom-call(s32[160]{0:T(256)} %order_ref.1, bf16[1,8,64,10240]{3,2,1,0:T(8,128)(2,1)} %grad_in.1, f32[2,5,512,512]{3,2,1,0:T(8,128)} %bitcast.12, bf16[2,5,512,512]{3,2,1,0:T(8,128)(2,1)} %bitcast.13), custom_call_target="tpu_custom_call" | custom-call | flops 13421772800 | bytes 104857600 | tf_op jit(solution)/shard_map/pallas_call | solution.py:409
  327.9 0.0 copy-done.1
  327.9 0.0 copy-start
  327.9 4.0 %copy-done = bf16[5,4,512,512]{3,2,1,0:T(8,128)(2,1)S(1)} copy-done((bf16[5,4,512,512]{3,2,1,0:T(8,128)(2,1)S(1)}, bf16[5,4,512,512]{3,2,1,0:T(8,128)(2,1)}, u32[]{:S(2)}) %copy-start) | copy-done | bytes 10485784
  331.9 0.0 copy-start.2
  331.9 9.5 %shard_map.68 = bf16[8,64,10240]{2,1,0:T(8,128)(2,1)} custom-call(s32[160]{0:T(256)S(1)} %copy-done.1, bf16[160,64,512]{2,1,0:T(8,128)(2,1)S(1)} %bitcast.9), custom_call_target="tpu_custom_call" | custom-call | bytes 20971520 | tf_op jit(solution)/shard_map/pallas_call | solution.py:450
  341.4 0.0 copy-done.2
  341.4 4.1 %copy.11 = f32[2,5,1,1,512,512]{5,4,3,2,1,0:T(8,128)} copy(f32[2,5,1,1,512,512]{5,4,3,2,1,0:T(8,128)S(1)} %bitcast.10) | data formatting | bytes 20971520
  345.5 5.2 %copy.12 = bf16[2,5,1,1,512,512]{5,4,3,2,1,0:T(8,128)(2,1)} copy(bf16[2,5,1,1,512,512]{5,4,3,2,1,0:T(8,128)(2,1)} %bitcast.11) | data formatting | bytes 10485760
Async XLA Ops:
  0.6 327.2 %copy-start.1 = (s32[160]{0:T(256)S(1)}, s32[160]{0:T(256)}, u32[]{:S(2)}) copy-start(s32[160]{0:T(256)} %order_ref.1) | copy-start | bytes 1924
  327.9 4.0 %copy-start = (bf16[5,4,512,512]{3,2,1,0:T(8,128)(2,1)S(1)}, bf16[5,4,512,512]{3,2,1,0:T(8,128)(2,1)}, u32[]{:S(2)}) copy-start(bf16[5,4,512,512]{3,2,1,0:T(8,128)(2,1)} %get-tuple-element.8) | copy-start | bytes 31457284
  331.9 9.5 %copy-start.2 = (f32[2,5,512,512]{3,2,1,0:T(8,128)S(1)}, f32[2,5,512,512]{3,2,1,0:T(8,128)}, u32[]{:S(2)}) copy-start(f32[2,5,512,512]{3,2,1,0:T(8,128)} %get-tuple-element.6) | copy-start | bytes 31457284
